TPU v7x, 512 devices: a whole 4x4x16 slice. The times are simulated.
512 devices in a mesh: var: 64 (over y, z_lo, core), ind: 8 (over x, z_hi).
Axes of the slice: x: 4, y: 4, z: 16 (z_hi: 2, z_lo: 8; z = z_hi * 8 + z_lo), core: 2. Of those that a mesh axis runs over, the one named last changes fastest.
Arguments:
- dosage: bfloat16 [16384, 32768], P('ind', 'var'), may hold values from 0 to 2
- positions: int32 [32768], replicated, may hold values from 10001 to 767829776, as said below
- partners: int32 [320], P('var'), may hold values from -1 to 63, as said below
Outputs:
- ld_tiles: bfloat16 [512, 320, 512], P('ind', 'var')
Inputs may be any that keep to these rules, and one draw needn't show every extreme that they name: positions strictly increase along the segment. `partners`: slot s of block k holds k + s when block k + s exists and its first variant lies within 3000000 base pairs of block k's last variant, else -1; slot 0 always holds k, so the -1 slots come last.
All inputs are finite; a program needn't handle non-finite values.
Results may differ from a plain program's by a relative error of at most 0.015.
Values may be sent and summed in bfloat16 or wider, within the bound.
A program may use at most 64 MiB of HBM per device.

v0:
```python
import jax
import jax.numpy as jnp
from jax import lax
from jax.sharding import PartitionSpec as P

WINDOW_BP = 3000000


def passed_along(shard, axis, by):
    devices = lax.axis_size(axis)
    pairs = [(i, i + by) for i in range(devices) if 0 <= i + by < devices]
    return lax.ppermute(shard, axis, pairs)


def per_device(dosage, positions, partners):
    row_count, block_width = dosage.shape
    group_count = lax.axis_size("ind")
    people = row_count * group_count
    var_index = lax.axis_index("var")
    group_index = lax.axis_index("ind")
    values = dosage.astype(jnp.float32)
    first_sum, second_sum = lax.psum(
        (jnp.sum(values, axis=0), jnp.sum(values * values, axis=0)), "ind"
    )
    average = first_sum / people
    spread = second_sum / people - average * average
    scaled = ((values - average) * lax.rsqrt(spread + 1e-06)).astype(jnp.bfloat16)
    slot_count = partners.shape[0]
    usable = partners >= 0

    def pair_tile(partner_block):
        result = jnp.einsum("nc,nb->cb", scaled, partner_block, preferred_element_type=jnp.float32)
        return result

    tile_list = [pair_tile(scaled)]
    current = scaled
    for offset in range(1, slot_count):
        current = passed_along(scaled, "var", -offset)
        tile_list.append(pair_tile(current))
    partial_tiles = jnp.stack(tile_list, axis=1)
    share_rows = block_width // group_count
    summed = lax.psum(partial_tiles.astype(jnp.bfloat16), "ind").astype(jnp.float32)
    own_rows = lax.dynamic_slice_in_dim(summed, group_index * share_rows, share_rows, 0)
    block_total = positions.shape[0] // block_width
    left_spots = lax.dynamic_slice_in_dim(
        positions, var_index * block_width + group_index * share_rows, share_rows
    )
    right_spots = jnp.stack(
        [
            lax.dynamic_slice_in_dim(
                positions,
                jnp.minimum(var_index + offset, block_total - 1) * block_width,
                block_width,
            )
            for offset in range(slot_count)
        ],
        axis=0,
    )
    inside = jnp.abs(right_spots[None, :, :] - left_spots[:, None, None]) <= WINDOW_BP
    kept_mask = inside & usable[None, :, None]
    return jnp.where(kept_mask, own_rows / people, jnp.float32(0.0)).astype(jnp.bfloat16)


def solution(mesh):
    return jax.shard_map(
        per_device,
        mesh=mesh,
        in_specs=(P("ind", "var"), P(), P("var")),
        out_specs=P("ind", "var", None),
        check_vma=False,
    )
```

profile of v0, /device:TPU:16, one launch (start us, length us, event | category | flops | bytes accessed | tf_op | source)
XLA Modules:
  0.0 744.3 jit_solution(7945160471586869663)
XLA Ops:
  6.5 0.0 all-reduce.3.cloned.1.call-start
  6.5 2.3 convert_reduce_fusion
  8.9 49.5 %all-reduce = (f32[512]{0:T(512)S(1)}, f32[512]{0:T(512)S(1)}) all-reduce(f32[512]{0:T(512)S(1)} %get-tuple-element.6, f32[512]{0:T(512)S(1)} %get-tuple-element.5), channel_id=1, replica_groups=mesh['var'=64,'ind'=8] {'ind'}, use_global_device_ids=true, to_apply=%region_3.0 | all-reduce | flops 1024 | bytes 8192 | tf_op jit(solution)/shard_map/psum | solution.py:22
  58.4 0.5 fusion.1
  58.9 1.9 collective-permute-start
  60.8 5.5 collective-permute-start.1
  66.4 2.3 collective-permute-start.2
  68.7 4.6 collective-permute-start.3
  73.2 1.3 fusion.4
  74.5 27.2 %collective-permute-done = bf16[2048,512]{1,0:T(8,128)(2,1)S(1)} collective-permute-done((bf16[2048,512]{1,0:T(8,128)(2,1)S(1)}, bf16[2048,512]{1,0:T(8,128)(2,1)S(1)}, u32[]{:S(2)}, u32[]{:S(2)}) %collective-permute-start) | collective-permute-done | bytes 2097184 | tf_op jit(solution)/shard_map/ppermute | solution.py:12
  101.7 1.3 fusion.6
  103.0 47.8 %collective-permute-done.1 = bf16[2048,512]{1,0:T(8,128)(2,1)S(1)} collective-permute-done((bf16[2048,512]{1,0:T(8,128)(2,1)S(1)}, bf16[2048,512]{1,0:T(8,128)(2,1)S(1)}, u32[]{:S(2)}, u32[]{:S(2)}) %collective-permute-start.1) | collective-permute-done | bytes 2097184 | tf_op jit(solution)/shard_map/ppermute | solution.py:12
  150.8 1.3 fusion.8
  152.0 39.6 %collective-permute-done.2 = bf16[2048,512]{1,0:T(8,128)(2,1)S(1)} collective-permute-done((bf16[2048,512]{1,0:T(8,128)(2,1)S(1)}, bf16[2048,512]{1,0:T(8,128)(2,1)S(1)}, u32[]{:S(2)}, u32[]{:S(2)}) %collective-permute-start.2) | collective-permute-done | bytes 2097184 | tf_op jit(solution)/shard_map/ppermute | solution.py:12
  191.6 1.3 fusion.10
  192.9 95.6 %collective-permute-done.3 = bf16[2048,512]{1,0:T(8,128)(2,1)S(1)} collective-permute-done((bf16[2048,512]{1,0:T(8,128)(2,1)S(1)}, bf16[2048,512]{1,0:T(8,128)(2,1)S(1)}, u32[]{:S(2)}, u32[]{:S(2)}) %collective-permute-start.3) | collective-permute-done | bytes 2097184 | tf_op jit(solution)/shard_map/ppermute | solution.py:12
  288.6 1.3 fusion.12
  289.9 0.0 copy-start.2
  289.9 1.5 copy-done.1
  291.4 0.0 all-reduce.3.cloned.1.call-update
  291.4 0.8 dynamic_slice.26
  292.2 0.8 fusion.14
  293.1 442.4 %all-reduce.3.cloned.1.call-done = bf16[512,5,512]{2,0,1:T(8,128)(2,1)} async-done(((bf16[512,5,512]{2,0,1:T(8,128)(2,1)}), bf16[512,5,512]{2,0,1:T(8,128)(2,1)}) %all-reduce.3.cloned.1.call-update) | async-done | bytes 2621456 | tf_op jit(solution)/shard_map/psum | solution.py:42
  735.5 2.0 select_convert_fusion
  (7 shorter events, 0.1 us)
Async XLA Ops:
  6.5 51.8 %copy-start = (bf16[2048,512]{1,0:T(8,128)(2,1)S(1)}, bf16[2048,512]{1,0:T(8,128)(2,1)}, u32[]{:S(2)}) copy-start(bf16[2048,512]{1,0:T(8,128)(2,1)} %param.3) | copy-start | bytes 6291460
  6.5 728.9 %all-reduce.3.cloned.1.call-start = ((), (), s32[]{:S(2)}) async-start(), calls=%async_computation | async-start | bytes 5242880 | tf_op jit(solution)/shard_map/psum | solution.py:42
  58.9 42.8 %collective-permute-start = (bf16[2048,512]{1,0:T(8,128)(2,1)S(1)}, bf16[2048,512]{1,0:T(8,128)(2,1)S(1)}, u32[]{:S(2)}, u32[]{:S(2)}) collective-permute-start(bf16[2048,512]{1,0:T(8,128)(2,1)S(1)} %fusion.1), channel_id=1, source_target_pairs={{8,0},{16,8},{24,16},{32,24},{40,32},{48,40},{56,48},{64,56},{72,6... | collective-permute-start | bytes 6291464 | tf_op jit(solution)/shard_map/ppermute | solution.py:12
  60.8 89.9 %collective-permute-start.1 = (bf16[2048,512]{1,0:T(8,128)(2,1)S(1)}, bf16[2048,512]{1,0:T(8,128)(2,1)S(1)}, u32[]{:S(2)}, u32[]{:S(2)}) collective-permute-start(bf16[2048,512]{1,0:T(8,128)(2,1)S(1)} %fusion.1), channel_id=1, source_target_pairs={{16,0},{24,8},{32,16},{40,24},{48,32},{56,40},{64,48},{72,56},{80,... | collective-permute-start | bytes 6291464 | tf_op jit(solution)/shard_map/ppermute | solution.py:12
  66.4 125.3 %collective-permute-start.2 = (bf16[2048,512]{1,0:T(8,128)(2,1)S(1)}, bf16[2048,512]{1,0:T(8,128)(2,1)S(1)}, u32[]{:S(2)}, u32[]{:S(2)}) collective-permute-start(bf16[2048,512]{1,0:T(8,128)(2,1)S(1)} %fusion.1), channel_id=1, source_target_pairs={{24,0},{32,8},{40,16},{48,24},{56,32},{64,40},{72,48},{80,56},{88,... | collective-permute-start | bytes 6291464 | tf_op jit(solution)/shard_map/ppermute | solution.py:12
  68.7 219.9 %collective-permute-start.3 = (bf16[2048,512]{1,0:T(8,128)(2,1)S(1)}, bf16[2048,512]{1,0:T(8,128)(2,1)S(1)}, u32[]{:S(2)}, u32[]{:S(2)}) collective-permute-start(bf16[2048,512]{1,0:T(8,128)(2,1)S(1)} %fusion.1), channel_id=1, source_target_pairs={{32,0},{40,8},{48,16},{56,24},{64,32},{72,40},{80,48},{88,56},{96,... | collective-permute-start | bytes 6291464 | tf_op jit(solution)/shard_map/ppermute | solution.py:12
  289.8 1.5 copy-start.1
  289.9 3.2 copy-start.2
Sparse Core Ops, SparseCore 0:
  291.5 443.9 all-reduce.2
where the time goes:
time: 745 us; the launch traced here: 744 us
  waiting for transfers between devices  653 us (88%)
  blocking collectives  49.5 us (7%)
  starting transfers between devices  14.3 us (2%)
  between operations  13.5 us (2%)
    psum x1, waiting for transfers between devices, per_device(): lax.psum(partial_tiles.astype(jnp.bfloat16), 'ind').astype(jnp.float32)  442 us
    ppermute x4, waiting for transfers between devices, passed_along(): return lax.ppermute(shard, axis, pairs)  210 us
    psum x1, blocking collectives, per_device(): lax.psum((jnp.sum(values, axis=0), jnp.sum(values * values, axis=0)), 'ind')  49.5 us
  transfers between devices with their start and end apart: 5, of which 5 were waited for; matrix products, arithmetic and copies ran while one was open for 1% of the time, Pallas kernels for 0%

commit v1 on v0

v1 whole, which is shorter than its diff:
```python
import jax
import jax.numpy as jnp
from jax import lax
from jax.experimental import pallas as pl
from jax.experimental.pallas import tpu as pltpu
from jax.sharding import PartitionSpec as P

WINDOW_BP = 3000000
MESH = pl.DeviceIdType.MESH

CHUNKS = 4
WIDE = 128
SLAB = 256


def kernel(
    dosage, out, raw, stats, left, pair, partial, from_x, to_z, kept, from_z, mom, mom_x, mom_z,
    load_sem, d_send, d_recv, r_send, r_recv, t_send, t_recv, u_send, u_recv,
    m_send, m_recv, x_send, x_recv, z_send, z_recv,
):
    v, i = lax.axis_index("var"), lax.axis_index("ind")
    rows = dosage.shape[0]
    blocks = lax.axis_size("var")
    people = rows * lax.axis_size("ind")
    core = lax.rem(v, 2)
    x, zh = lax.div(i, 2), lax.rem(i, 2)
    below = (jnp.maximum(v - 2, 0), i)
    above = (jnp.minimum(v + 2, blocks - 1), i)
    sibling = (v + 1 - 2 * core, i)
    opposite = (v, i + 1 - 2 * zh)

    def x_peer(d):
        return lax.rem(x + d, 4)

    has_below, has_above, has_above2 = v >= 2, v + 2 < blocks, lax.div(v, 2) + 2 < lax.div(blocks, 2)

    barrier = pltpu.get_barrier_semaphore()
    for d in (1, 2, 3):
        pl.semaphore_signal(barrier, inc=1, device_id=(v, 2 * x_peer(d) + zh), device_id_type=MESH)
    pl.semaphore_signal(barrier, inc=1, device_id=sibling, device_id_type=MESH)
    pl.semaphore_signal(barrier, inc=1, device_id=opposite, device_id_type=MESH)

    @pl.when(has_below)
    def _():
        pl.semaphore_signal(barrier, inc=1, device_id=below, device_id_type=MESH)

    @pl.when(has_above)
    def _():
        pl.semaphore_signal(barrier, inc=1, device_id=above, device_id_type=MESH)

    def load(j):
        return pltpu.make_async_copy(dosage.at[:, pl.ds(j * WIDE, WIDE)], raw.at[0, j], load_sem.at[j])

    for j in range(CHUNKS):
        load(j).start()

    greeted = 5 + jnp.minimum(lax.div(v, 2), 1) + jnp.minimum(lax.div(blocks - 1 - v, 2), 1)
    pl.semaphore_wait(barrier, greeted)

    def remote(src, dst, send, recv, to):
        return pltpu.make_async_remote_copy(
            src_ref=src, dst_ref=dst, send_sem=send, recv_sem=recv, device_id=to, device_id_type=MESH
        )

    def send_own(j):
        return remote(raw.at[0, j], raw.at[2, j], d_send.at[0, j], d_recv.at[0, j], below)

    def forward(j):
        return remote(raw.at[2, j], raw.at[4, j], d_send.at[1, j], d_recv.at[1, j], below)

    def second(phase):
        return 3 - 2 * core if phase == 0 else 1 + 2 * core

    def passed(phase):
        return 2 if phase == 0 else 4 - 4 * core

    def sibling_second(phase):
        return 1 + 2 * core if phase == 0 else 3 - 2 * core

    def relay(phase, j):
        return remote(
            raw.at[passed(phase), j], raw.at[sibling_second(phase), j], r_send.at[phase, j], r_recv.at[phase, j], sibling
        )

    def relay_arrival(phase, j):
        return remote(raw.at[0, j], raw.at[second(phase), j], r_send.at[phase, j], r_recv.at[phase, j], sibling)

    def stats_send(phase):
        return remote(stats.at[2 * phase], stats.at[2 + 2 * phase], t_send.at[phase], t_recv.at[phase], below)

    def stats_relay(phase):
        return remote(
            stats.at[passed(phase)], stats.at[sibling_second(phase)], u_send.at[phase], u_recv.at[phase], sibling
        )

    def stats_relay_arrival(phase):
        return remote(stats.at[0], stats.at[second(phase)], u_send.at[phase], u_recv.at[phase], sibling)

    arrives = [has_above, has_above2]
    relays = [has_above, (core == 1) | has_above2]
    relayed = [has_above, (core == 0) | has_above2]

    for j in range(CHUNKS):
        load(j).wait()

        @pl.when(has_below)
        def _():
            send_own(j).start()

    for j in range(CHUNKS):

        def add_up(n, totals):
            part = raw[0, j, pl.ds(pl.multiple_of(n * SLAB, SLAB), SLAB), :].astype(jnp.float32)
            return totals[0] + jnp.sum(part, axis=0, keepdims=True), totals[1] + jnp.sum(
                part * part, axis=0, keepdims=True
            )

        zero = jnp.zeros((1, WIDE), jnp.float32)
        first, squares = lax.fori_loop(0, rows // SLAB, add_up, (zero, zero))
        mom[j, 0:1, :] = first
        mom[j, 1:2, :] = squares
        mom[j, 2:8, :] = jnp.zeros((6, WIDE), jnp.float32)

    def moments_x(d):
        return remote(mom, mom_x.at[d - 1], m_send.at[d - 1], m_recv.at[d - 1], (v, 2 * x_peer(d) + zh))

    for d in (2, 1, 3):
        moments_x(d).start()
    for d in (1, 2, 3):
        moments_x(d).wait_recv()
    mom_z[0] = (mom[...] + mom_x[1]) + (mom_x[0] + mom_x[2])
    moments_z = remote(mom_z.at[0], mom_z.at[1], m_send.at[3], m_recv.at[3], opposite)
    moments_z.start()
    moments_z.wait_recv()
    total = mom_z[0] + mom_z[1]
    average = total[:, 0:1, :] / people
    spread = total[:, 1:2, :] / people - average * average
    stats[0, :, 0:1, :] = average
    stats[0, :, 1:2, :] = lax.rsqrt(spread + 1e-06)
    stats[0, :, 2:8, :] = jnp.zeros((CHUNKS, 6, WIDE), jnp.float32)

    @pl.when(has_below)
    def _():
        stats_send(0).start()

    def scale(slot, j, column):
        average = stats[slot, j, 0:1, :]
        inverse = stats[slot, j, 1:2, :]

        def body(n, carry):
            where = pl.ds(pl.multiple_of(n * SLAB, SLAB), SLAB)
            values = raw[slot, j, where, :].astype(jnp.float32)
            pair[where, pl.ds(column * WIDE, WIDE)] = ((values - average) * inverse).astype(jnp.bfloat16)
            return carry

        lax.fori_loop(0, rows // SLAB, body, 0)

    def turn(column, j):
        def body(n, carry):
            where = pl.ds(pl.multiple_of(n * SLAB, SLAB), SLAB)
            part = pair[where, pl.ds(column * WIDE, WIDE)]
            left[pl.ds(j * WIDE, WIDE), where] = part.T
            return carry

        lax.fori_loop(0, rows // SLAB, body, 0)

    def share_x(t, d):
        to = x_peer(d)
        return remote(
            partial.at[t, pl.ds(pl.multiple_of(to * 128, 128), 128)], from_x.at[t, d - 1],
            x_send.at[t, d - 1], x_recv.at[t, d - 1], (v, 2 * to + zh),
        )

    def share_z(t):
        return remote(to_z.at[t], from_z.at[t], z_send.at[t], z_recv.at[t], opposite)

    def multiply(t):
        partial[t] = jnp.dot(left[...], pair[...], preferred_element_type=jnp.float32).astype(jnp.bfloat16)
        for d in (2, 1, 3):
            share_x(t, d).start()

    def half(t, which):
        own = pl.ds(pl.multiple_of(x * 128 + which * 64, 64), 64)
        there = pl.ds(pl.multiple_of(which * 64, 64), 64)
        return (partial[t, own, :].astype(jnp.float32) + from_x[t, 1, there, :].astype(jnp.float32)) + (
            from_x[t, 0, there, :].astype(jnp.float32) + from_x[t, 2, there, :].astype(jnp.float32)
        )

    def reduce(t):
        for d in (1, 2, 3):
            share_x(t, d).wait_recv()
        to_z[t] = half(t, 1 - zh).astype(jnp.bfloat16)
        share_z(t).start()
        kept[t] = half(t, zh)

    def finish(t, first_slot, first_chunk, second_slot, second_chunk):
        share_z(t).wait_recv()
        total = (kept[t] + from_z[t].astype(jnp.float32)) / people
        out[first_slot, first_chunk] = total[:, :WIDE]
        out[second_slot, second_chunk] = total[:, WIDE:]

    for t in (1, 0):
        for column in range(2):
            scale(0, 2 * t + column, column)
            turn(column, 2 * t + column)
    multiply(0)
    for column in range(2):
        scale(0, 2 + column, column)
    multiply(1)
    for t in range(2):
        reduce(t)

    for phase in range(2):

        @pl.when(arrives[phase])
        def _():
            stats_send(phase).wait_recv()

        if phase == 0:

            @pl.when(has_below & has_above)
            def _():
                stats_send(1).start()

        @pl.when(relays[phase])
        def _():
            stats_relay(phase).start()

        @pl.when(relayed[phase])
        def _():
            stats_relay_arrival(phase).wait_recv()

        def step(j, carry):
            @pl.when(arrives[phase])
            def _():
                (send_own if phase == 0 else forward)(j).wait_recv()

            if phase == 0:

                @pl.when(has_below & has_above)
                def _():
                    forward(j).start()

            @pl.when(relays[phase])
            def _():
                relay(phase, j).start()

            scale(2 + 2 * phase, j, 0)

            @pl.when(relayed[phase])
            def _():
                relay_arrival(phase, j).wait_recv()

            scale(second(phase), j, 1)
            t = 2 + 4 * phase + j
            multiply(t)
            reduce(t)
            return carry

        lax.fori_loop(0, CHUNKS, step, 0)

    for t in range(2):
        finish(t, 0, 2 * t, 0, 2 * t + 1)
    for phase in range(2):

        def last(j, carry):
            finish(2 + 4 * phase + j, 2 + 2 * phase, j, second(phase), j)
            return carry

        lax.fori_loop(0, CHUNKS, last, 0)

    for d in (1, 2, 3):
        moments_x(d).wait_send()
    moments_z.wait_send()

    @pl.when(has_below)
    def _():
        stats_send(0).wait_send()

    @pl.when(has_below & has_above)
    def _():
        stats_send(1).wait_send()

    for phase in range(2):

        @pl.when(relays[phase])
        def _():
            stats_relay(phase).wait_send()

    def drain(j, carry):
        @pl.when(has_below)
        def _():
            send_own(j).wait_send()

        @pl.when(has_below & has_above)
        def _():
            forward(j).wait_send()

        for phase in range(2):

            @pl.when(relays[phase])
            def _():
                relay(phase, j).wait_send()

        return carry

    lax.fori_loop(0, CHUNKS, drain, 0)

    def drain_sums(t, carry):
        for d in (1, 2, 3):
            share_x(t, d).wait_send()
        share_z(t).wait_send()
        return carry

    lax.fori_loop(0, 2 + 2 * CHUNKS, drain_sums, 0)


def sums(dosage):
    rows, width = dosage.shape
    steps = 2 + 2 * CHUNKS
    dma = pltpu.SemaphoreType.DMA
    return pl.pallas_call(
        kernel,
        out_shape=jax.ShapeDtypeStruct((5, CHUNKS, 64, WIDE), jnp.float32),
        in_specs=[pl.BlockSpec(memory_space=pl.ANY)],
        out_specs=pl.BlockSpec(memory_space=pltpu.VMEM),
        scratch_shapes=[
            pltpu.VMEM((5, CHUNKS, rows, WIDE), jnp.bfloat16),
            pltpu.VMEM((5, CHUNKS, 8, WIDE), jnp.float32),
            pltpu.VMEM((width, rows), jnp.bfloat16),
            pltpu.VMEM((rows, 2 * WIDE), jnp.bfloat16),
            pltpu.VMEM((steps, width, 2 * WIDE), jnp.bfloat16),
            pltpu.VMEM((steps, 3, 128, 2 * WIDE), jnp.bfloat16),
            pltpu.VMEM((steps, 64, 2 * WIDE), jnp.bfloat16),
            pltpu.VMEM((steps, 64, 2 * WIDE), jnp.float32),
            pltpu.VMEM((steps, 64, 2 * WIDE), jnp.bfloat16),
            pltpu.VMEM((CHUNKS, 8, WIDE), jnp.float32),
            pltpu.VMEM((3, CHUNKS, 8, WIDE), jnp.float32),
            pltpu.VMEM((2, CHUNKS, 8, WIDE), jnp.float32),
            dma((CHUNKS,)),
            dma((2, CHUNKS)), dma((2, CHUNKS)), dma((2, CHUNKS)), dma((2, CHUNKS)),
            dma((2,)), dma((2,)), dma((2,)), dma((2,)),
            dma((4,)), dma((4,)),
            dma((steps, 3)), dma((steps, 3)), dma((steps,)), dma((steps,)),
        ],
        compiler_params=pltpu.CompilerParams(
            collective_id=0, has_side_effects=True, vmem_limit_bytes=48 * 2**20
        ),
    )(dosage)


def per_device(dosage, positions, partners):
    block_width = dosage.shape[1]
    group_count = lax.axis_size("ind")
    var_index = lax.axis_index("var")
    group_index = lax.axis_index("ind")
    slot_count = partners.shape[0]
    usable = partners >= 0
    share_rows = block_width // group_count
    correlation = sums(dosage).transpose(2, 0, 1, 3).reshape(share_rows, slot_count, block_width)
    block_total = positions.shape[0] // block_width
    left_spots = lax.dynamic_slice_in_dim(
        positions, var_index * block_width + group_index * share_rows, share_rows
    )
    right_spots = jnp.stack(
        [
            lax.dynamic_slice_in_dim(
                positions,
                jnp.minimum(var_index + offset, block_total - 1) * block_width,
                block_width,
            )
            for offset in range(slot_count)
        ],
        axis=0,
    )
    inside = jnp.abs(right_spots[None, :, :] - left_spots[:, None, None]) <= WINDOW_BP
    kept_mask = inside & usable[None, :, None]
    return jnp.where(kept_mask, correlation, jnp.float32(0.0)).astype(jnp.bfloat16)


def solution(mesh):
    return jax.shard_map(
        per_device,
        mesh=mesh,
        in_specs=(P("ind", "var"), P(), P("var")),
        out_specs=P("ind", "var", None),
        check_vma=False,
    )
```

time: 745 us -> 167 us (0.22)
  the two profiles are of different devices: /device:TPU:16 before, /device:TPU:120 now
where the time goes in v1:
time: 167 us
  Pallas kernels  162 us (97%)
  local copies, waits for them, and re-layouts  3.22 us (2%)
  other arithmetic  1.68 us (1%)
    pallas_call x1, Pallas kernels, sums(): pl.pallas_call(kernel, out_shape=jax.ShapeDtypeStruct((5, CHUNKS, 64, WID...  162 us

profile of v1, /device:TPU:120, one launch (start us, length us, event | category | flops | bytes accessed | tf_op | source)
XLA Modules:
  0.0 166.7 jit_solution(13435620825850493014)
XLA Ops:
  0.0 0.8 dynamic_slice.23
  0.8 0.7 broadcast_compare_fusion
  1.4 0.8 fusion.2
  2.3 0.0 copy-start
  2.3 1.6 copy-done
  3.9 161.8 %shard_map.37 = f32[5,4,64,128]{3,2,1,0:T(8,128)S(1)} custom-call(bf16[2048,512]{1,0:T(8,128)(2,1)S(1)} %copy-done), custom_call_target="tpu_custom_call" | custom-call | tf_op jit(solution)/shard_map/pallas_call | solution.py:322
  165.7 1.0 fusion
  (1 shorter events, 0.0 us)
Async XLA Ops:
  2.3 1.6 copy-start

commit v2 on v1

--- a/solution.py
+++ b/solution.py
@@ -14,7 +14,7 @@
 
 
 def kernel(
-    dosage, out, raw, stats, left, pair, partial, from_x, to_z, kept, from_z, mom, mom_x, mom_z,
+    dosage, positions, partners, out, raw, stats, left, pair, partial, from_x, to_z, kept, from_z, mom, mom_x, mom_z, spots,
     load_sem, d_send, d_recv, r_send, r_recv, t_send, t_recv, u_send, u_recv,
     m_send, m_recv, x_send, x_recv, z_send, z_recv,
 ):
@@ -102,10 +102,11 @@
 
     for j in range(CHUNKS):
         load(j).wait()
-
-        @pl.when(has_below)
-        def _():
-            send_own(j).start()
+        if j < CHUNKS // 2:
+
+            @pl.when(has_below)
+            def _():
+                send_own(j).start()
 
     for j in range(CHUNKS):
 
@@ -142,6 +143,11 @@
     @pl.when(has_below)
     def _():
         stats_send(0).start()
+        for j in range(CHUNKS // 2, CHUNKS):
+            send_own(j).start()
+
+    line = positions[pl.ds(4 * v + x, 1), :]
+    spots[...] = jnp.broadcast_to(line, (128, 128)).T
 
     def scale(slot, j, column):
         average = stats[slot, j, 0:1, :]
@@ -196,8 +202,12 @@
     def finish(t, first_slot, first_chunk, second_slot, second_chunk):
         share_z(t).wait_recv()
         total = (kept[t] + from_z[t].astype(jnp.float32)) / people
-        out[first_slot, first_chunk] = total[:, :WIDE]
-        out[second_slot, second_chunk] = total[:, WIDE:]
+        own_spots = spots[pl.ds(pl.multiple_of(zh * 64, 64), 64), :]
+        for column, slot, chunk in ((0, first_slot, first_chunk), (1, second_slot, second_chunk)):
+            place = jnp.minimum(v + slot, blocks - 1) * CHUNKS + chunk
+            inside = jnp.abs(positions[pl.ds(place, 1), :] - own_spots) <= WINDOW_BP
+            usable = jnp.where(inside, partners[slot], -1) >= 0
+            out[slot, chunk] = jnp.where(usable, total[:, column * WIDE : (column + 1) * WIDE], 0.0)
 
     for t in (1, 0):
         for column in range(2):
@@ -207,8 +217,7 @@
     for column in range(2):
         scale(0, 2 + column, column)
     multiply(1)
-    for t in range(2):
-        reduce(t)
+    reduce(0)
 
     for phase in range(2):
 
@@ -254,13 +263,14 @@
             scale(second(phase), j, 1)
             t = 2 + 4 * phase + j
             multiply(t)
-            reduce(t)
+            reduce(t - 1)
             return carry
 
         lax.fori_loop(0, CHUNKS, step, 0)
 
     for t in range(2):
         finish(t, 0, 2 * t, 0, 2 * t + 1)
+    reduce(1 + 2 * CHUNKS)
     for phase in range(2):
 
         def last(j, carry):
@@ -315,14 +325,18 @@
     lax.fori_loop(0, 2 + 2 * CHUNKS, drain_sums, 0)
 
 
-def sums(dosage):
+def tiles(dosage, positions, partners):
     rows, width = dosage.shape
     steps = 2 + 2 * CHUNKS
     dma = pltpu.SemaphoreType.DMA
     return pl.pallas_call(
         kernel,
         out_shape=jax.ShapeDtypeStruct((5, CHUNKS, 64, WIDE), jnp.float32),
-        in_specs=[pl.BlockSpec(memory_space=pl.ANY)],
+        in_specs=[
+            pl.BlockSpec(memory_space=pl.ANY),
+            pl.BlockSpec(memory_space=pltpu.VMEM),
+            pl.BlockSpec(memory_space=pltpu.SMEM),
+        ],
         out_specs=pl.BlockSpec(memory_space=pltpu.VMEM),
         scratch_shapes=[
             pltpu.VMEM((5, CHUNKS, rows, WIDE), jnp.bfloat16),
@@ -337,6 +351,7 @@
             pltpu.VMEM((CHUNKS, 8, WIDE), jnp.float32),
             pltpu.VMEM((3, CHUNKS, 8, WIDE), jnp.float32),
             pltpu.VMEM((2, CHUNKS, 8, WIDE), jnp.float32),
+            pltpu.VMEM((128, 128), jnp.int32),
             dma((CHUNKS,)),
             dma((2, CHUNKS)), dma((2, CHUNKS)), dma((2, CHUNKS)), dma((2, CHUNKS)),
             dma((2,)), dma((2,)), dma((2,)), dma((2,)),
@@ -344,38 +359,15 @@
             dma((steps, 3)), dma((steps, 3)), dma((steps,)), dma((steps,)),
         ],
         compiler_params=pltpu.CompilerParams(
-            collective_id=0, has_side_effects=True, vmem_limit_bytes=48 * 2**20
+            collective_id=0, has_side_effects=True, vmem_limit_bytes=60 * 2**20
         ),
-    )(dosage)
+    )(dosage, positions.reshape(-1, WIDE), partners)
 
 
 def per_device(dosage, positions, partners):
-    block_width = dosage.shape[1]
-    group_count = lax.axis_size("ind")
-    var_index = lax.axis_index("var")
-    group_index = lax.axis_index("ind")
-    slot_count = partners.shape[0]
-    usable = partners >= 0
-    share_rows = block_width // group_count
-    correlation = sums(dosage).transpose(2, 0, 1, 3).reshape(share_rows, slot_count, block_width)
-    block_total = positions.shape[0] // block_width
-    left_spots = lax.dynamic_slice_in_dim(
-        positions, var_index * block_width + group_index * share_rows, share_rows
-    )
-    right_spots = jnp.stack(
-        [
-            lax.dynamic_slice_in_dim(
-                positions,
-                jnp.minimum(var_index + offset, block_total - 1) * block_width,
-                block_width,
-            )
-            for offset in range(slot_count)
-        ],
-        axis=0,
-    )
-    inside = jnp.abs(right_spots[None, :, :] - left_spots[:, None, None]) <= WINDOW_BP
-    kept_mask = inside & usable[None, :, None]
-    return jnp.where(kept_mask, correlation, jnp.float32(0.0)).astype(jnp.bfloat16)
+    masked = tiles(dosage, positions, partners)
+    share_rows = masked.shape[2]
+    return masked.transpose(2, 0, 1, 3).reshape(share_rows, partners.shape[0], dosage.shape[1]).astype(jnp.bfloat16)
 
 
 def solution(mesh):

time: 167 us -> 160 us (0.958)
  the two profiles are of different devices: /device:TPU:120 before, /device:TPU:59 now
where the time goes in v2:
time: 160 us
  Pallas kernels  158 us (99%)
  other arithmetic  1.85 us (1%)
    pallas_call x1, Pallas kernels, tiles(): pl.pallas_call(kernel, out_shape=jax.ShapeDtypeStruct((5, CHUNKS, 64, WID...  158 us

profile of v2, /device:TPU:59, one launch (start us, length us, event | category | flops | bytes accessed | tf_op | source)
XLA Modules:
  0.0 159.9 jit_solution(15595851895495149189)
XLA Ops:
  0.0 158.1 %shard_map.37 = f32[5,4,64,128]{3,2,1,0:T(8,128)} custom-call(bf16[2048,512]{1,0:T(8,128)(2,1)} %dosage.1, s32[256,128]{1,0:T(8,128)} %bitcast.7, s32[5]{0:T(128)} %partners.1), custom_call_target="tpu_custom_call" | custom-call | tf_op jit(solution)/shard_map/pallas_call | solution.py:332
  158.1 1.9 %copy_bitcast_fusion = bf16[64,5,512]{2,0,1:T(8,128)(2,1)} fusion(f32[5,4,64,128]{3,2,1,0:T(8,128)} %shard_map.37), kind=kLoop, calls=%fused_computation | loop fusion | flops 163840 | bytes 983040 | tf_op jit(solution)/shard_map/convert_element_type | solution.py:370

commit v3 on v2

--- a/solution.py
+++ b/solution.py
@@ -14,7 +14,7 @@
 
 
 def kernel(
-    dosage, positions, partners, out, raw, stats, left, pair, partial, from_x, to_z, kept, from_z, mom, mom_x, mom_z, spots,
+    dosage, positions, partners, out, raw, stats, left, pair, partial, from_x, to_z, kept, from_z, mom, mom_x, mom_z, spots, along, down,
     load_sem, d_send, d_recv, r_send, r_recv, t_send, t_recv, u_send, u_recv,
     m_send, m_recv, x_send, x_recv, z_send, z_recv,
 ):
@@ -129,16 +129,20 @@
         moments_x(d).start()
     for d in (1, 2, 3):
         moments_x(d).wait_recv()
-    mom_z[0] = (mom[...] + mom_x[1]) + (mom_x[0] + mom_x[2])
+    half_people = people // 2
+
+    def half_scale(first, squares):
+        average = first / half_people
+        spread = jnp.maximum(squares / half_people - average * average, 0.0)
+        return average, spread + 1e-06
+
+    half_sums = (mom[...] + mom_x[1]) + (mom_x[0] + mom_x[2])
+    average, spread = half_scale(half_sums[:, 0:1, :], half_sums[:, 1:2, :])
+    stats[0, :, 0:1, :] = average
+    stats[0, :, 1:2, :] = lax.rsqrt(spread)
+    stats[0, :, 2:4, :] = half_sums[:, 0:2, :]
+    stats[0, :, 4:8, :] = jnp.zeros((CHUNKS, 4, WIDE), jnp.float32)
     moments_z = remote(mom_z.at[0], mom_z.at[1], m_send.at[3], m_recv.at[3], opposite)
-    moments_z.start()
-    moments_z.wait_recv()
-    total = mom_z[0] + mom_z[1]
-    average = total[:, 0:1, :] / people
-    spread = total[:, 1:2, :] / people - average * average
-    stats[0, :, 0:1, :] = average
-    stats[0, :, 1:2, :] = lax.rsqrt(spread + 1e-06)
-    stats[0, :, 2:8, :] = jnp.zeros((CHUNKS, 6, WIDE), jnp.float32)
 
     @pl.when(has_below)
     def _():
@@ -196,18 +200,33 @@
         for d in (1, 2, 3):
             share_x(t, d).wait_recv()
         to_z[t] = half(t, 1 - zh).astype(jnp.bfloat16)
-        share_z(t).start()
         kept[t] = half(t, zh)
 
     def finish(t, first_slot, first_chunk, second_slot, second_chunk):
         share_z(t).wait_recv()
-        total = (kept[t] + from_z[t].astype(jnp.float32)) / people
-        own_spots = spots[pl.ds(pl.multiple_of(zh * 64, 64), 64), :]
+        half_rows = pl.ds(pl.multiple_of(zh * 64, 64), 64)
+        own_spots = spots[half_rows, :]
         for column, slot, chunk in ((0, first_slot, first_chunk), (1, second_slot, second_chunk)):
             place = jnp.minimum(v + slot, blocks - 1) * CHUNKS + chunk
             inside = jnp.abs(positions[pl.ds(place, 1), :] - own_spots) <= WINDOW_BP
             usable = jnp.where(inside, partners[slot], -1) >= 0
-            out[slot, chunk] = jnp.where(usable, total[:, column * WIDE : (column + 1) * WIDE], 0.0)
+            lanes = slice(column * WIDE, (column + 1) * WIDE)
+            across = pl.ds(slot * CHUNKS + chunk, 1)
+            mine = kept[t, :, lanes] * down[0, half_rows, :] * along[0, across, :]
+            other = from_z[t, :, lanes].astype(jnp.float32) * down[1, half_rows, :] * along[1, across, :]
+            total = (mine + other) / people + down[2, half_rows, :] * along[2, across, :]
+            out[slot, chunk] = jnp.where(usable, total, 0.0)
+
+    def whole_statistics():
+        average, spread = half_scale(mom_z[0, 0], mom_z[0, 1])
+        other_spread = half_scale(mom_z[1, 0], mom_z[1, 1])[1]
+        mean = (mom_z[0, 0] + mom_z[1, 0]) / people
+        inverse = lax.rsqrt((mom_z[0, 1] + mom_z[1, 1]) / people - mean * mean + 1e-06)
+        along[0] = spread * lax.rsqrt(spread) * inverse
+        along[1] = other_spread * lax.rsqrt(other_spread) * inverse
+        along[2] = (average - mean) * inverse
+        for k in range(3):
+            down[k] = jnp.broadcast_to(along[k, pl.ds(x, 1), :], (128, 128)).T
 
     for t in (1, 0):
         for column in range(2):
@@ -239,6 +258,15 @@
         def _():
             stats_relay_arrival(phase).wait_recv()
 
+        if phase == 1:
+            for slot in range(5):
+                for j in range(CHUNKS):
+                    for row in range(2):
+                        mom_z[0, row, slot * CHUNKS + j : slot * CHUNKS + j + 1, :] = stats[
+                            slot, j, 2 + row : 3 + row, :
+                        ]
+            mom_z[0, :, 20:24, :] = jnp.zeros((2, 4, WIDE), jnp.float32)
+
         def step(j, carry):
             @pl.when(arrives[phase])
             def _():
@@ -253,6 +281,18 @@
             @pl.when(relays[phase])
             def _():
                 relay(phase, j).start()
+
+            if phase == 1:
+
+                @pl.when(j == 3)
+                def _():
+                    moments_z.start()
+
+                    def held(u, carry):
+                        share_z(u).start()
+                        return carry
+
+                    lax.fori_loop(0, 8, held, 0)
 
             scale(2 + 2 * phase, j, 0)
 
@@ -264,13 +304,22 @@
             t = 2 + 4 * phase + j
             multiply(t)
             reduce(t - 1)
+            if phase == 1:
+
+                @pl.when(j == 3)
+                def _():
+                    share_z(t - 1).start()
+
             return carry
 
         lax.fori_loop(0, CHUNKS, step, 0)
 
+    reduce(1 + 2 * CHUNKS)
+    share_z(1 + 2 * CHUNKS).start()
+    moments_z.wait_recv()
+    whole_statistics()
     for t in range(2):
         finish(t, 0, 2 * t, 0, 2 * t + 1)
-    reduce(1 + 2 * CHUNKS)
     for phase in range(2):
 
         def last(j, carry):
@@ -350,8 +399,10 @@
             pltpu.VMEM((steps, 64, 2 * WIDE), jnp.bfloat16),
             pltpu.VMEM((CHUNKS, 8, WIDE), jnp.float32),
             pltpu.VMEM((3, CHUNKS, 8, WIDE), jnp.float32),
-            pltpu.VMEM((2, CHUNKS, 8, WIDE), jnp.float32),
+            pltpu.VMEM((2, 2, 24, WIDE), jnp.float32),
             pltpu.VMEM((128, 128), jnp.int32),
+            pltpu.VMEM((3, 24, WIDE), jnp.float32),
+            pltpu.VMEM((3, 128, 128), jnp.float32),
             dma((CHUNKS,)),
             dma((2, CHUNKS)), dma((2, CHUNKS)), dma((2, CHUNKS)), dma((2, CHUNKS)),
             dma((2,)), dma((2,)), dma((2,)), dma((2,)),

time: 160 us -> 149 us (0.931)
  the two profiles are of different devices: /device:TPU:59 before, /device:TPU:440 now
where the time goes in v3:
time: 149 us; the launch traced here: 148 us
  Pallas kernels  147 us (99%)
  other arithmetic  1.85 us (1%)
    pallas_call x1, Pallas kernels, tiles(): pl.pallas_call(kernel, out_shape=jax.ShapeDtypeStruct((5, CHUNKS, 64, WID...  147 us

profile of v3, /device:TPU:440, one launch (start us, length us, event | category | flops | bytes accessed | tf_op | source)
XLA Modules:
  0.0 148.4 jit_solution(2439791792095026476)
XLA Ops:
  0.0 146.6 %shard_map.37 = f32[5,4,64,128]{3,2,1,0:T(8,128)} custom-call(bf16[2048,512]{1,0:T(8,128)(2,1)} %dosage.1, s32[256,128]{1,0:T(8,128)} %bitcast.7, s32[5]{0:T(128)} %partners.1), custom_call_target="tpu_custom_call" | custom-call | tf_op jit(solution)/shard_map/pallas_call | solution.py:381
  146.6 1.9 %copy_bitcast_fusion = bf16[64,5,512]{2,0,1:T(8,128)(2,1)} fusion(f32[5,4,64,128]{3,2,1,0:T(8,128)} %shard_map.37), kind=kLoop, calls=%fused_computation | loop fusion | flops 163840 | bytes 983040 | tf_op jit(solution)/shard_map/convert_element_type | solution.py:421

commit v4 on v3

--- a/solution.py
+++ b/solution.py
@@ -142,7 +142,17 @@
     stats[0, :, 1:2, :] = lax.rsqrt(spread)
     stats[0, :, 2:4, :] = half_sums[:, 0:2, :]
     stats[0, :, 4:8, :] = jnp.zeros((CHUNKS, 4, WIDE), jnp.float32)
-    moments_z = remote(mom_z.at[0], mom_z.at[1], m_send.at[3], m_recv.at[3], opposite)
+    moments_z = remote(mom_z.at[0, x], mom_z.at[1, x], m_send.at[3], m_recv.at[3], opposite)
+
+    def moments_back(d):
+        return remote(
+            mom_z.at[1, x], mom_z.at[1, x], m_send.at[3 + d], m_recv.at[3 + d], (v, 2 * x_peer(d) + zh)
+        )
+
+    def moments_back_arrival(d):
+        there = mom_z.at[1, x_peer(4 - d)]
+        return remote(there, there, m_send.at[3 + d], m_recv.at[3 + d], (v, 2 * x_peer(d) + zh))
+
 
     @pl.when(has_below)
     def _():
@@ -211,22 +221,22 @@
             inside = jnp.abs(positions[pl.ds(place, 1), :] - own_spots) <= WINDOW_BP
             usable = jnp.where(inside, partners[slot], -1) >= 0
             lanes = slice(column * WIDE, (column + 1) * WIDE)
-            across = pl.ds(slot * CHUNKS + chunk, 1)
-            mine = kept[t, :, lanes] * down[0, half_rows, :] * along[0, across, :]
-            other = from_z[t, :, lanes].astype(jnp.float32) * down[1, half_rows, :] * along[1, across, :]
-            total = (mine + other) / people + down[2, half_rows, :] * along[2, across, :]
+            across = pl.ds(slot, 1)
+            mine = kept[t, :, lanes] * down[0, half_rows, :] * along[0, chunk, across, :]
+            other = from_z[t, :, lanes].astype(jnp.float32) * down[1, half_rows, :] * along[1, chunk, across, :]
+            total = (mine + other) / people + down[2, half_rows, :] * along[2, chunk, across, :]
             out[slot, chunk] = jnp.where(usable, total, 0.0)
 
     def whole_statistics():
-        average, spread = half_scale(mom_z[0, 0], mom_z[0, 1])
-        other_spread = half_scale(mom_z[1, 0], mom_z[1, 1])[1]
-        mean = (mom_z[0, 0] + mom_z[1, 0]) / people
-        inverse = lax.rsqrt((mom_z[0, 1] + mom_z[1, 1]) / people - mean * mean + 1e-06)
+        average, spread = half_scale(mom_z[0, :, 0], mom_z[0, :, 1])
+        other_spread = half_scale(mom_z[1, :, 0], mom_z[1, :, 1])[1]
+        mean = (mom_z[0, :, 0] + mom_z[1, :, 0]) / people
+        inverse = lax.rsqrt((mom_z[0, :, 1] + mom_z[1, :, 1]) / people - mean * mean + 1e-06)
         along[0] = spread * lax.rsqrt(spread) * inverse
         along[1] = other_spread * lax.rsqrt(other_spread) * inverse
         along[2] = (average - mean) * inverse
         for k in range(3):
-            down[k] = jnp.broadcast_to(along[k, pl.ds(x, 1), :], (128, 128)).T
+            down[k] = jnp.broadcast_to(along[k, x, 0:1, :], (128, 128)).T
 
     for t in (1, 0):
         for column in range(2):
@@ -262,10 +272,8 @@
             for slot in range(5):
                 for j in range(CHUNKS):
                     for row in range(2):
-                        mom_z[0, row, slot * CHUNKS + j : slot * CHUNKS + j + 1, :] = stats[
-                            slot, j, 2 + row : 3 + row, :
-                        ]
-            mom_z[0, :, 20:24, :] = jnp.zeros((2, 4, WIDE), jnp.float32)
+                        mom_z[0, j, row, slot : slot + 1, :] = stats[slot, j, 2 + row : 3 + row, :]
+            mom_z[0, :, :, 5:8, :] = jnp.zeros((CHUNKS, 2, 3, WIDE), jnp.float32)
 
         def step(j, carry):
             @pl.when(arrives[phase])
@@ -317,6 +325,10 @@
     reduce(1 + 2 * CHUNKS)
     share_z(1 + 2 * CHUNKS).start()
     moments_z.wait_recv()
+    for d in (1, 2, 3):
+        moments_back(d).start()
+    for d in (1, 2, 3):
+        moments_back_arrival(d).wait_recv()
     whole_statistics()
     for t in range(2):
         finish(t, 0, 2 * t, 0, 2 * t + 1)
@@ -331,6 +343,8 @@
     for d in (1, 2, 3):
         moments_x(d).wait_send()
     moments_z.wait_send()
+    for d in (1, 2, 3):
+        moments_back(d).wait_send()
 
     @pl.when(has_below)
     def _():
@@ -399,14 +413,14 @@
             pltpu.VMEM((steps, 64, 2 * WIDE), jnp.bfloat16),
             pltpu.VMEM((CHUNKS, 8, WIDE), jnp.float32),
             pltpu.VMEM((3, CHUNKS, 8, WIDE), jnp.float32),
-            pltpu.VMEM((2, 2, 24, WIDE), jnp.float32),
+            pltpu.VMEM((2, CHUNKS, 2, 8, WIDE), jnp.float32),
             pltpu.VMEM((128, 128), jnp.int32),
-            pltpu.VMEM((3, 24, WIDE), jnp.float32),
+            pltpu.VMEM((3, CHUNKS, 8, WIDE), jnp.float32),
             pltpu.VMEM((3, 128, 128), jnp.float32),
             dma((CHUNKS,)),
             dma((2, CHUNKS)), dma((2, CHUNKS)), dma((2, CHUNKS)), dma((2, CHUNKS)),
             dma((2,)), dma((2,)), dma((2,)), dma((2,)),
-            dma((4,)), dma((4,)),
+            dma((7,)), dma((7,)),
             dma((steps, 3)), dma((steps, 3)), dma((steps,)), dma((steps,)),
         ],
         compiler_params=pltpu.CompilerParams(

time: 149 us -> 147 us (0.987)
  Pallas kernels: 147 us -> 145 us
where the time goes in v4:
time: 147 us
  Pallas kernels  145 us (99%)
  other arithmetic  1.85 us (1%)
    pallas_call x1, Pallas kernels, tiles(): pl.pallas_call(kernel, out_shape=jax.ShapeDtypeStruct((5, CHUNKS, 64, WID...  145 us

profile of v4, /device:TPU:440, one launch (start us, length us, event | category | flops | bytes accessed | tf_op | source)
XLA Modules:
  0.0 147.1 jit_solution(7759586276000106401)
XLA Ops:
  0.0 145.2 %shard_map.37 = f32[5,4,64,128]{3,2,1,0:T(8,128)} custom-call(bf16[2048,512]{1,0:T(8,128)(2,1)} %dosage.1, s32[256,128]{1,0:T(8,128)} %bitcast.7, s32[5]{0:T(128)} %partners.1), custom_call_target="tpu_custom_call" | custom-call | tf_op jit(solution)/shard_map/pallas_call | solution.py:395
  145.2 1.9 %copy_bitcast_fusion = bf16[64,5,512]{2,0,1:T(8,128)(2,1)} fusion(f32[5,4,64,128]{3,2,1,0:T(8,128)} %shard_map.37), kind=kLoop, calls=%fused_computation | loop fusion | flops 163840 | bytes 983040 | tf_op jit(solution)/shard_map/convert_element_type | solution.py:435

commit v5 on v4

--- a/solution.py
+++ b/solution.py
@@ -16,7 +16,7 @@
 def kernel(
     dosage, positions, partners, out, raw, stats, left, pair, partial, from_x, to_z, kept, from_z, mom, mom_x, mom_z, spots, along, down,
     load_sem, d_send, d_recv, r_send, r_recv, t_send, t_recv, u_send, u_recv,
-    m_send, m_recv, x_send, x_recv, z_send, z_recv,
+    m_send, m_recv, x_send, x_recv, z_send, z_recv, go,
 ):
     v, i = lax.axis_index("var"), lax.axis_index("ind")
     rows = dosage.shape[0]
@@ -33,6 +33,8 @@
         return lax.rem(x + d, 4)
 
     has_below, has_above, has_above2 = v >= 2, v + 2 < blocks, lax.div(v, 2) + 2 < lax.div(blocks, 2)
+
+    chip, chips = lax.div(v, 2), lax.div(blocks, 2)
 
     barrier = pltpu.get_barrier_semaphore()
     for d in (1, 2, 3):
@@ -294,6 +296,14 @@
 
                 @pl.when(j == 3)
                 def _():
+                    @pl.when(chip + 2 >= chips)
+                    def _():
+                        pl.semaphore_wait(go, 1)
+
+                    @pl.when((chip + 3 >= chips) & has_above)
+                    def _():
+                        pl.semaphore_signal(go, inc=1, device_id=above, device_id_type=MESH)
+
                     moments_z.start()
 
                     def held(u, carry):
@@ -422,6 +432,7 @@
             dma((2,)), dma((2,)), dma((2,)), dma((2,)),
             dma((7,)), dma((7,)),
             dma((steps, 3)), dma((steps, 3)), dma((steps,)), dma((steps,)),
+            pltpu.SemaphoreType.REGULAR,
         ],
         compiler_params=pltpu.CompilerParams(
             collective_id=0, has_side_effects=True, vmem_limit_bytes=60 * 2**20

time: 147 us -> 143 us (0.973)
  the two profiles are of different devices: /device:TPU:440 before, /device:TPU:56 now
where the time goes in v5:
time: 143 us
  Pallas kernels  141 us (99%)
  other arithmetic  1.85 us (1%)
    pallas_call x1, Pallas kernels, tiles(): pl.pallas_call(kernel, out_shape=jax.ShapeDtypeStruct((5, CHUNKS, 64, WID...  141 us

profile of v5, /device:TPU:56, one launch (start us, length us, event | category | flops | bytes accessed | tf_op | source)
XLA Modules:
  0.0 142.6 jit_solution(6316102848936319648)
XLA Ops:
  0.0 140.7 %shard_map.37 = f32[5,4,64,128]{3,2,1,0:T(8,128)} custom-call(bf16[2048,512]{1,0:T(8,128)(2,1)} %dosage.1, s32[256,128]{1,0:T(8,128)} %bitcast.7, s32[5]{0:T(128)} %partners.1), custom_call_target="tpu_custom_call" | custom-call | tf_op jit(solution)/shard_map/pallas_call | solution.py:405
  140.8 1.9 %copy_bitcast_fusion = bf16[64,5,512]{2,0,1:T(8,128)(2,1)} fusion(f32[5,4,64,128]{3,2,1,0:T(8,128)} %shard_map.37), kind=kLoop, calls=%fused_computation | loop fusion | flops 163840 | bytes 983040 | tf_op jit(solution)/shard_map/convert_element_type | solution.py:446
